TPU v7x, 32 devices: a whole 2x2x4 slice. The times are simulated.
32 devices in a mesh: energy: 8 (over y, x, core), layer: 4 (over z).
Axes of the slice: x: 2, y: 2, z: 4, core: 2. Of those that a mesh axis runs over, the one named last changes fastest.
Arguments:
- green_blocks: bfloat16 [32, 4, 2, 384, 384], P('energy', 'layer'), may hold values from -6 to 6
- offsets: int32 [4], replicated, may hold values from -4 to 4, as said below
- occupation: float32 [4], replicated, may hold values from 0.1 to 2
- coupling: int32 [4, 4], P('layer'), may hold values from 0 to 3
- vertex: bfloat16 [4, 2, 384, 384], replicated, may hold values from -0.15625 to 0.15625
- magnon_free: bfloat16 [4, 2, 384, 384], replicated, may hold values from -0.0068359375 to 0.0068359375
Outputs:
- sigma: bfloat16 [32, 4, 2, 384, 384], P('energy', 'layer')
Inputs may be any that keep to these rules, and one draw needn't show every extreme that they name: `offsets`: each offset is a nonzero whole number; one equals 4 and one equals -4.
All inputs are finite; a program needn't handle non-finite values.
Results may differ from a plain program's by a relative error of at most 0.0056.
Values may be sent and summed in bfloat16 or wider, within the bound.
A program may use at most 192 MiB of HBM per device.

v0:
```python
import jax
import jax.numpy as jnp
from jax import lax
from jax.sharding import PartitionSpec as P


def padded_2(block, sides, width):
    for axis, dim in sides:
        count = lax.axis_size(axis)
        forward = [(i, i + 1) for i in range(count - 1)]
        backward = [(target, source) for source, target in forward]
        low = lax.ppermute(
            lax.slice_in_dim(block, block.shape[dim] - width, None, axis=dim), axis, forward
        )
        high = lax.ppermute(lax.slice_in_dim(block, 0, width, axis=dim), axis, backward)
        block = jnp.concatenate([low, block, high], axis=dim)
    return block


def complex_mul(pattern, left_real, left_imag, right_real, right_imag):

    def product(first, second):
        return jnp.einsum(pattern, first, second, preferred_element_type=jnp.float32)

    return (
        product(left_real, right_real) - product(left_imag, right_imag),
        product(left_real, right_imag) + product(left_imag, right_real),
    )


def per_device(green_blocks, offsets, occupation, coupling, vertex, magnon_free):
    count = green_blocks.shape[0]
    padded = padded_2(green_blocks, (("energy", 0),), count)
    local_index = jnp.arange(count, dtype=jnp.int32)[:, None]
    below = jnp.take(padded, local_index + count - offsets[None, :], axis=0)
    above = jnp.take(padded, local_index + count + offsets[None, :], axis=0)
    below_wide = below.astype(jnp.float32)
    above_wide = above.astype(jnp.float32)
    chosen = vertex[coupling]
    weights = occupation[None, :, None, None, None, None]
    mixed = (weights * below_wide + (weights + 1.0) * above_wide).astype(jnp.bfloat16)
    half_real, half_imag = complex_mul(
        "gkab,ekgbc->ekgac", chosen[:, :, 0], chosen[:, :, 1], mixed[:, :, :, 0], mixed[:, :, :, 1]
    )
    half_real = half_real.astype(jnp.bfloat16)
    half_imag = half_imag.astype(jnp.bfloat16)
    born_real, born_imag = complex_mul(
        "ekgab,gkcb->egac", half_real, half_imag, chosen[:, :, 0], -chosen[:, :, 1]
    )
    own_wide = green_blocks.astype(jnp.float32)[:, None]
    flipped = jnp.swapaxes(above_wide, -1, -2)
    polar_real = jnp.sum(
        own_wide[:, :, :, 0] * flipped[:, :, :, 0] - own_wide[:, :, :, 1] * flipped[:, :, :, 1],
        axis=(0, 2),
    )
    polar_imag = jnp.sum(
        own_wide[:, :, :, 0] * flipped[:, :, :, 1] + own_wide[:, :, :, 1] * flipped[:, :, :, 0],
        axis=(0, 2),
    )
    partial_polar = jnp.stack([polar_real, polar_imag], axis=1)
    polar_full = lax.psum(partial_polar, ("energy", "layer")).astype(jnp.bfloat16)
    full_real, full_imag = complex_mul(
        "kab,kbc->kac", polar_full[:, 0], polar_full[:, 1], magnon_free[:, 0], magnon_free[:, 1]
    )
    magnon = jnp.stack([full_real, full_imag], axis=1).astype(jnp.bfloat16)
    magnon_wide = magnon.astype(jnp.float32)
    summed = below_wide + above_wide
    hadamard_real = jnp.sum(
        magnon_wide[None, :, None, 0] * summed[:, :, :, 0]
        - magnon_wide[None, :, None, 1] * summed[:, :, :, 1],
        axis=1,
    )
    hadamard_imag = jnp.sum(
        magnon_wide[None, :, None, 0] * summed[:, :, :, 1]
        + magnon_wide[None, :, None, 1] * summed[:, :, :, 0],
        axis=1,
    )
    return jnp.stack([born_real + hadamard_real, born_imag + hadamard_imag], axis=2).astype(
        jnp.bfloat16
    )


def solution(mesh):
    placed = (P("energy", "layer", None, None, None), P(), P(), P("layer", None), P(), P())
    return jax.shard_map(
        per_device,
        mesh=mesh,
        in_specs=placed,
        out_specs=P("energy", "layer", None, None, None),
        check_vma=False,
    )
```

profile of v0, /device:TPU:0, one launch (start us, length us, event | category | flops | bytes accessed | tf_op | source)
XLA Modules:
  0.0 315.6 jit_solution(9487727184855456967)
XLA Ops:
  0.0 0.0 copy-start
  0.0 3.9 %collective-permute-start = (bf16[4,1,2,384,384]{4,3,2,1,0:T(8,128)(2,1)}, bf16[4,1,2,384,384]{4,3,2,1,0:T(8,128)(2,1)}, u32[]{:S(2)}, u32[]{:S(2)}) collective-permute-start(bf16[4,1,2,384,384]{4,3,2,1,0:T(8,128)(2,1)} %param.8), channel_id=1, source_target_pairs={{0,4},{4,8},{8,12},{12,16},{16,20},{20,24},{24,28},{1,5},{5,9},{9,... | collective-permute-start | bytes 7077896 | tf_op jit(solution)/shard_map/ppermute | solution.py:12
  3.9 1.3 collective-permute-start.1
  5.2 0.7 compare_select_fusion
  5.9 0.1 reshape.295
  6.0 0.7 compare_and_fusion
  6.7 0.1 copy.21
  6.9 0.1 reshape.290
  6.9 0.1 copy.19
  7.0 0.7 fusion.38
  7.7 2.3 gather_fusion
  10.0 2.1 copy.49
  12.1 0.3 copy-done.8
  12.4 0.3 bitcast_convert_fusion
  12.7 2.6 slice_bitcast_fusion.17
  15.3 0.0 collective-permute-done
  15.3 0.0 collective-permute-done.1
  15.3 5.9 %maximum_bitcast_fusion = bf16[12,2,384,384]{3,2,1,0:T(8,128)(2,1)} fusion(bf16[4,1,2,384,384]{4,3,2,1,0:T(8,128)(2,1)} %collective-permute-done.1, bf16[4,1,2,384,384]{4,3,2,1,0:T(8,128)(2,1)S(1)} %copy-done.8, bf16[4,1,2,384,384]{4,3,2,1,0:T(8,128)(2,1)} %collective-permute-done), kind=kLoop, calls=%fused_computation.21 | loop fusion | flops 7077888 | bytes 14155776 | tf_op jit(solution)/shard_map/jit(_take)/Arg_0.3 | solution.py:35
  21.2 8.6 %gather_fusion.2 = bf16[16,2,384,384]{3,2,1,0:T(8,128)(2,1)} fusion(bf16[12,2,384,384]{3,2,1,0:T(8,128)(2,1)} %maximum_bitcast_fusion, s32[1024]{0:T(1024)S(1)} %pad_clamp_fusion), kind=kCustom, calls=%fused_computation.1.clone | custom fusion | bytes 18874432 | tf_op jit(solution)/shard_map/jit(_take)/gather | solution.py:36
  29.9 12.7 %copy.22 = bf16[4,4,1,2,384,384]{4,5,0,1,3,2:T(8,128)(2,1)} copy(bf16[4,4,1,2,384,384]{5,4,3,1,0,2:T(8,128)(2,1)} %bitcast.213) | data formatting | bytes 18874368 | tf_op jit(solution)/shard_map/jit(_take)/gather | solution.py:36
  42.6 11.5 %convert_bitcast_fusion = f32[4,4,1,2,384,384]{5,4,0,1,3,2:T(8,128)} fusion(bf16[4,4,1,2,384,384]{4,5,0,1,3,2:T(8,128)(2,1)} %copy.22, pred[4,4]{0,1:T(4,128)(4,1)S(1)} %copy.21), kind=kLoop, calls=%fused_computation.4 | loop fusion | flops 9437184 | bytes 28311568 | tf_op jit(solution)/shard_map/transpose | solution.py:51
  54.0 9.3 %subtract_reduce_fusion.1 = (f32[4,384,384]{2,1,0:T(8,128)S(1)}, f32[4,384,384]{2,1,0:T(8,128)S(1)}) fusion(f32[4,4,1,2,384,384]{5,4,0,1,3,2:T(8,128)} %convert_bitcast_fusion, f32[4,384,384]{2,1,0:T(8,128)} %get-tuple-element.15, f32[4,384,384]{2,1,0:T(8,128)} %get-tuple-element.14), kind=kLoop, calls=%fused_computation.16 | loop fusion | flops 17694720 | bytes 28311552 | tf_op jit(solution)/shard_map/reduce_sum | solution.py:52
  63.4 2.5 pad_maximum_fusion
  65.8 141.0 %all-reduce.1 = bf16[4,2,384,384]{3,2,0,1:T(8,128)(2,1)} all-reduce(f32[4,2,384,384]{3,2,0,1:T(8,128)} %pad_maximum_fusion), channel_id=1, replica_groups=mesh['energy'=8,'layer'=4] {'energy','layer'}, use_global_device_ids=true, to_apply=%region_2.4 | all-reduce | flops 1179648 | bytes 7077888 | tf_op jit(solution)/shard_map/psum | solution.py:61
  206.8 4.0 %fusion.25 = f32[4,384,384]{2,1,0:T(8,128)} fusion(bf16[4,2,384,384]{3,2,0,1:T(8,128)(2,1)} %all-reduce.1, bf16[4,2,384,384]{3,2,1,0:T(8,128)(2,1)} %param.13), kind=kOutput, calls=%fused_computation.63 | convolution fusion | flops 452984832 | bytes 4718592 | tf_op jit(solution)/shard_map/kab,kbc->kac/dot_general | solution.py:23
  210.8 2.3 fusion.21
  213.2 8.6 %gather_fusion.1 = bf16[16,2,384,384]{3,2,1,0:T(8,128)(2,1)} fusion(bf16[12,2,384,384]{3,2,1,0:T(8,128)(2,1)} %maximum_bitcast_fusion, s32[1024]{0:T(1024)S(1)} %pad_clamp_fusion.1), kind=kCustom, calls=%fused_computation.clone | custom fusion | bytes 18874432 | tf_op jit(solution)/shard_map/jit(_take)/gather | solution.py:35
  221.8 12.7 %copy.20 = bf16[4,4,1,2,384,384]{4,5,0,1,3,2:T(8,128)(2,1)} copy(bf16[4,4,1,2,384,384]{5,4,3,1,0,2:T(8,128)(2,1)} %bitcast.212) | data formatting | bytes 18874368 | tf_op jit(solution)/shard_map/jit(_take)/gather | solution.py:35
  234.5 14.5 %fusion.1 = (bf16[4,4,1,2,384,384]{4,5,0,1,3,2:T(8,128)(2,1)S(1)}, f32[4,4,1,2,384,384]{4,5,0,1,3,2:T(8,128)}) fusion(f32[4]{0:T(128)S(1)} %broadcast_add_fusion, f32[4]{0:T(128)S(1)} %copy-done.13, bf16[4,4,1,2,384,384]{4,5,0,1,3,2:T(8,128)(2,1)} %copy.20, pred[4,4]{0,1:T(4,128)(4,1)S(1)} %copy.19, bf16[4,4,1,2,384,384]{4,5,0,1,3,2:T(8,128)(2,1)} %copy.22, ...), kind=kLoop, calls=%fused_computation.8 | loop fusion | flops 42467328 | bytes 47185984 | tf_op jit(solution)/shard_map/convert_element_type | solution.py:41
  249.0 6.0 %fusion.5 = f32[4,4,384,384]{3,2,1,0:T(8,128)} fusion(bf16[4,4,1,2,384,384]{4,5,0,1,3,2:T(8,128)(2,1)S(1)} %get-tuple-element.10, bf16[1,4,2,384,384]{4,3,1,2,0:T(8,128)(2,1)S(1)} %bitcast.214), kind=kOutput, calls=%fused_computation.28 | convolution fusion | flops 1811939328 | bytes 15335424 | tf_op jit(solution)/shard_map/gkab,ekgbc->ekgac/dot_general | solution.py:23
  255.0 5.4 %fusion.4 = f32[4,4,384,384]{3,2,1,0:T(8,128)} fusion(bf16[4,4,1,2,384,384]{4,5,0,1,3,2:T(8,128)(2,1)S(1)} %get-tuple-element.10, bf16[1,4,2,384,384]{4,3,1,2,0:T(8,128)(2,1)S(1)} %bitcast.215), kind=kOutput, calls=%fused_computation.27 | convolution fusion | flops 1811939328 | bytes 15335424 | tf_op jit(solution)/shard_map/gkab,ekgbc->ekgac/dot_general | solution.py:23
  260.5 6.9 %fusion.2 = bf16[4,4,384,384]{2,3,0,1:T(8,128)(2,1)} fusion(f32[4,4,384,384]{3,2,1,0:T(8,128)} %fusion.5, bf16[4,4,1,2,384,384]{4,5,0,1,3,2:T(8,128)(2,1)S(1)} %get-tuple-element.10, bf16[1,4,2,384,384]{4,3,1,2,0:T(8,128)(2,1)S(1)} %bitcast.216), kind=kOutput, calls=%fused_computation.22 | convolution fusion | flops 1816657920 | bytes 20054016 | tf_op jit(solution)/shard_map/gkab,ekgbc->ekgac/dot_general | solution.py:23
  267.4 5.9 %fusion.33 = f32[384,4,384,1]{2,0,1,3:T(8,128)} fusion(bf16[4,4,384,384]{2,3,0,1:T(8,128)(2,1)} %fusion.2, bf16[1,4,2,384,384]{4,3,1,2,0:T(8,128)(2,1)S(1)} %bitcast.217), kind=kOutput, calls=%fused_computation.72 | convolution fusion | flops 1811939328 | bytes 8257536 | tf_op jit(solution)/shard_map/ekgab,gkcb->egac/dot_general | solution.py:23
  273.3 3.5 %fusion.18 = f32[384,4,384,1]{2,0,1,3:T(8,128)} fusion(bf16[4,4,384,384]{2,3,0,1:T(8,128)(2,1)S(1)} %copy-done.5, bf16[1,4,2,384,384]{4,3,1,2,0:T(8,128)(2,1)S(1)} %bitcast.218), kind=kOutput, calls=%fused_computation.56 | convolution fusion | flops 1813708800 | bytes 8257536 | tf_op jit(solution)/shard_map/ekgab,gkcb->egac/dot_general | solution.py:23
  276.8 0.9 fusion.16
  277.7 0.8 copy-done.9
  278.5 0.9 fusion.17
  279.4 0.3 maximum_convert_fusion
  279.7 2.6 slice_bitcast_fusion.15
  282.3 3.1 copy.27
  285.3 3.0 copy.28
  288.4 8.3 %fusion.3 = bf16[4,4,384,384]{2,3,0,1:T(8,128)(2,1)S(1)} fusion(f32[4,4,384,384]{3,2,1,0:T(8,128)} %fusion.4, bf16[4,4,1,2,384,384]{4,5,0,1,3,2:T(8,128)(2,1)} %copy-done.2, bf16[1,4,2,384,384]{4,3,1,2,0:T(8,128)(2,1)S(1)} %bitcast.219), kind=kOutput, calls=%fused_computation.23 | convolution fusion | flops 1816657920 | bytes 20054016 | tf_op jit(solution)/shard_map/gkab,ekgbc->ekgac/dot_general | solution.py:23
  296.7 8.7 %subtract_reduce_fusion = (f32[4,384,384]{1,2,0:T(8,128)S(1)}, f32[4,384,384]{1,2,0:T(8,128)S(1)}) fusion(f32[4,4,1,2,384,384]{4,5,0,1,3,2:T(8,128)} %get-tuple-element.11, f32[4,384,384]{1,2,0:T(8,128)S(1)} %copy-done.7, f32[4,384,384]{1,2,0:T(8,128)S(1)} %copy-done.6), kind=kLoop, calls=%fused_computation.14 | loop fusion | flops 17694720 | bytes 28311552 | tf_op jit(solution)/shard_map/reduce_sum | solution.py:68
  305.5 2.1 fusion.14
  307.5 2.1 fusion.15
  309.6 0.0 copy-start.1
  309.7 1.7 pad_maximum_fusion.1
  311.3 4.3 %copy.31 = bf16[4,1,2,384,384]{4,3,2,1,0:T(8,128)(2,1)} copy(bf16[4,1,2,384,384]{3,4,0,2,1:T(8,128)(2,1)} %pad_maximum_fusion.1) | data formatting | bytes 4718592 | tf_op jit(solution)/shard_map/stack | solution.py:78
  (33 shorter events, 0.1 us)
Async XLA Ops:
  0.0 7.7 %copy-start = (bf16[4,2,384,384]{3,2,1,0:T(8,128)(2,1)S(1)}, bf16[4,2,384,384]{3,2,1,0:T(8,128)(2,1)}, u32[]{:S(2)}) copy-start(bf16[4,2,384,384]{3,2,1,0:T(8,128)(2,1)} %param.12) | copy-start | bytes 7077892
  0.0 15.3 %collective-permute-start = (bf16[4,1,2,384,384]{4,3,2,1,0:T(8,128)(2,1)}, bf16[4,1,2,384,384]{4,3,2,1,0:T(8,128)(2,1)}, u32[]{:S(2)}, u32[]{:S(2)}) collective-permute-start(bf16[4,1,2,384,384]{4,3,2,1,0:T(8,128)(2,1)} %param.8), channel_id=1, source_target_pairs={{0,4},{4,8},{8,12},{12,16},{16,20},{20,24},{24,28},{1,5},{5,9},{9,... | collective-permute-start | bytes 7077896 | tf_op jit(solution)/shard_map/ppermute | solution.py:12
  3.9 11.4 %collective-permute-start.1 = (bf16[4,1,2,384,384]{4,3,2,1,0:T(8,128)(2,1)}, bf16[4,1,2,384,384]{4,3,2,1,0:T(8,128)(2,1)}, u32[]{:S(2)}, u32[]{:S(2)}) collective-permute-start(bf16[4,1,2,384,384]{4,3,2,1,0:T(8,128)(2,1)} %param.8), channel_id=1, source_target_pairs={{4,0},{8,4},{12,8},{16,12},{20,16},{24,20},{28,24},{5,1},{9,5},{13... | collective-permute-start | bytes 7077896 | tf_op jit(solution)/shard_map/ppermute | solution.py:15
  10.0 2.1 copy-start.13
  10.0 2.4 copy-start.8
  206.8 4.0 %copy-start.3 = (bf16[4,2,384,384]{3,2,0,1:T(8,128)(2,1)S(1)}, bf16[4,2,384,384]{3,2,0,1:T(8,128)(2,1)}, u32[]{:S(2)}) copy-start(bf16[4,2,384,384]{3,2,0,1:T(8,128)(2,1)} %all-reduce.1) | copy-start | bytes 7077892
  206.8 4.0 %copy-start.11 = (bf16[4,2,384,384]{3,2,1,0:T(8,128)(2,1)S(1)}, bf16[4,2,384,384]{3,2,1,0:T(8,128)(2,1)}, u32[]{:S(2)}) copy-start(bf16[4,2,384,384]{3,2,1,0:T(8,128)(2,1)} %param.13) | copy-start | bytes 7077892
  249.0 11.4 %copy-start.2 = (bf16[4,4,1,2,384,384]{4,5,0,1,3,2:T(8,128)(2,1)}, bf16[4,4,1,2,384,384]{4,5,0,1,3,2:T(8,128)(2,1)S(1)}, u32[]{:S(2)}) copy-start(bf16[4,4,1,2,384,384]{4,5,0,1,3,2:T(8,128)(2,1)S(1)} %get-tuple-element.10) | copy-start | bytes 28311556
  267.4 5.9 %copy-start.5 = (bf16[4,4,384,384]{2,3,0,1:T(8,128)(2,1)S(1)}, bf16[4,4,384,384]{2,3,0,1:T(8,128)(2,1)}, u32[]{:S(2)}) copy-start(bf16[4,4,384,384]{2,3,0,1:T(8,128)(2,1)} %fusion.2) | copy-start | bytes 14155780
  273.3 3.5 %copy-start.4 = (bf16[4,2,384,384]{3,2,0,1:T(8,128)(2,1)S(1)}, bf16[4,2,384,384]{3,2,0,1:T(8,128)(2,1)}, u32[]{:S(2)}) copy-start(bf16[4,2,384,384]{3,2,0,1:T(8,128)(2,1)} %all-reduce.1) | copy-start | bytes 7077892
  273.3 3.5 %copy-start.10 = (f32[4,384,384]{2,1,0:T(8,128)S(1)}, f32[4,384,384]{2,1,0:T(8,128)}, u32[]{:S(2)}) copy-start(f32[4,384,384]{2,1,0:T(8,128)} %fusion.25) | copy-start | bytes 7077892
  273.3 3.5 %copy-start.12 = (bf16[4,2,384,384]{3,2,1,0:T(8,128)(2,1)S(1)}, bf16[4,2,384,384]{3,2,1,0:T(8,128)(2,1)}, u32[]{:S(2)}) copy-start(bf16[4,2,384,384]{3,2,1,0:T(8,128)(2,1)} %param.13) | copy-start | bytes 7077892
  276.8 1.7 copy-start.9
  288.4 8.3 %copy-start.6 = (f32[4,384,384]{1,2,0:T(8,128)S(1)}, f32[4,384,384]{1,2,0:T(8,128)}, u32[]{:S(2)}) copy-start(f32[4,384,384]{1,2,0:T(8,128)} %copy.27) | copy-start | bytes 7077892
  288.4 8.3 %copy-start.7 = (f32[4,384,384]{1,2,0:T(8,128)S(1)}, f32[4,384,384]{1,2,0:T(8,128)}, u32[]{:S(2)}) copy-start(f32[4,384,384]{1,2,0:T(8,128)} %copy.28) | copy-start | bytes 7077892
  296.7 8.7 %copy-start.14 = (f32[384,4,384,1]{2,0,1,3:T(8,128)S(1)}, f32[384,4,384,1]{2,0,1,3:T(8,128)}, u32[]{:S(2)}) copy-start(f32[384,4,384,1]{2,0,1,3:T(8,128)} %fusion.33) | copy-start | bytes 7077892
  305.5 2.1 copy-start.15
  309.6 6.0 %copy-start.1 = (bf16[4,2,384,384]{3,2,1,0:T(8,128)(2,1)S(1)}, bf16[4,2,384,384]{3,2,1,0:T(8,128)(2,1)}, u32[]{:S(2)}) copy-start(bf16[4,2,384,384]{3,2,1,0:T(8,128)(2,1)} %param.12) | copy-start | bytes 7077892
where the time goes:
time: 317 us; the launch traced here: 316 us
  blocking collectives  141 us (44%)
  local copies, waits for them, and re-layouts  64 us (20%)
  other arithmetic  56.9 us (18%)
  matrix products  48.3 us (15%)
  starting transfers between devices  5.18 us (2%)
    psum x1, blocking collectives, per_device(): lax.psum(partial_polar, ('energy', 'layer')).astype(jnp.bfloat16)  141 us
    dot_general x12, matrix products, product(): jnp.einsum(pattern, first, second, preferred_element_type=jnp.float32)  48.3 us
    gather x2, local copies, waits for them, and re-layouts, per_device(): below = jnp.take(padded, local_index + count - offsets[None, :], axis=0)  21.3 us
    gather x2, local copies, waits for them, and re-layouts, per_device(): above = jnp.take(padded, local_index + count + offsets[None, :], axis=0)  21.3 us
    convert_element_type x1, other arithmetic, per_device(): (weights * below_wide + (weights + 1.0) * above_wide).astype(jnp.bfloat16)  14.5 us
    transpose x1, other arithmetic, per_device(): flipped = jnp.swapaxes(above_wide, -1, -2)  11.5 us
    reduce_sum x1, other arithmetic, per_device(): jnp.sum(own_wide[:, :, :, 0] * flipped[:, :, :, 0] - own_wide[:, :, :, 1]...  9.32 us
    reduce_sum x1, other arithmetic, per_device(): jnp.sum(magnon_wide[None, :, None, 0] * summed[:, :, :, 0] - magnon_wide[...  8.71 us
  transfers between devices with their start and end apart: 2, of which 0 were waited for; matrix products, arithmetic and copies ran while one was open for 3% of the time, Pallas kernels for 0%

commit v1 on v0

v1 whole, which is shorter than its diff:
```python
import functools

import jax
import jax.numpy as jnp
from jax import lax
from jax.experimental import pallas as pl
from jax.experimental.pallas import tpu as pltpu
from jax.sharding import PartitionSpec as P

MESH = pl.DeviceIdType.MESH
F32 = jnp.float32
BF16 = jnp.bfloat16
ROWS = 32
ALIGN = 16


def reduction_plan(n_energy, n_layer, rows):
    bits = []
    bit = 2
    while bit < n_energy:
        bits.append(bit)
        bit *= 2
    kinds = [[1, 1]] if n_energy > 1 else []
    if bits:
        kinds.append([bits[-1], bits[0]])
    kinds.append([0, 0])
    for i in range(1, len(bits)):
        kinds.append([bits[-1 - i], bits[i]])
    plan = []
    size = rows
    for pair in kinds:
        parts = n_layer if pair[0] == 0 else 2
        if parts == 1:
            continue
        split = size % (parts * ALIGN) == 0
        after = size // parts if split else size
        plan.append((pair, parts, split, size, after))
        size = after
    return plan


def kernel(
    n_energy, n_layer, plan,
    off_ref, occ_ref, coup_ref, green_ref, vertex_ref, free_ref, out_ref,
    lo, up, own_t, wide, wide_t, acc, mix, half, part, full, mag, reach, coef, *rest,
):
    count = green_ref.shape[0]
    nb = green_ref.shape[-1]
    noff = off_ref.shape[0]
    nq = noff - 1
    stages = len(plan)
    landing = rest[:stages]
    halo_send, halo_recv = rest[stages], rest[stages + 1]
    sums_send = rest[stages + 2:2 * stages + 2]
    sums_recv = rest[2 * stages + 2:3 * stages + 2]
    spread_send = rest[3 * stages + 2:4 * stages + 2]
    spread_recv = rest[4 * stages + 2:5 * stages + 2]

    me = lax.axis_index("energy")
    layer = lax.axis_index("layer")

    barrier = pltpu.get_barrier_semaphore()

    def greet(energy, group):
        pl.semaphore_signal(barrier, inc=1, device_id=(energy, group), device_id_type=MESH)

    def flipped(bit):
        return me + bit * (1 - 2 * (lax.div(me, bit) % 2))

    peers = [(lax.rem(me + 1, n_energy), layer), (lax.rem(me + n_energy - 1, n_energy), layer)]
    for bit in sorted({b for pair, _, _, _, _ in plan for b in pair if b > 1}):
        peers.append((flipped(bit), layer))
    for r in range(1, n_layer):
        peers.append((me, lax.rem(layer + r, n_layer)))
    for peer in peers:
        greet(*peer)
    pl.semaphore_wait(barrier, len(peers))

    def send_next(e):
        return pltpu.make_async_remote_copy(
            src_ref=green_ref.at[e], dst_ref=lo.at[e], send_sem=halo_send.at[0, e],
            recv_sem=halo_recv.at[0, e], device_id=(me + 1, layer), device_id_type=MESH)

    def send_prev(e):
        return pltpu.make_async_remote_copy(
            src_ref=green_ref.at[e], dst_ref=up.at[count + e], send_sem=halo_send.at[1, e],
            recv_sem=halo_recv.at[1, e], device_id=(me - 1, layer), device_id_type=MESH)

    @pl.when(me > 0)
    def _():
        for e in range(count):
            send_prev(e).start()

    @pl.when(me < n_energy - 1)
    def _():
        for e in range(count):
            send_next(e).start()

    @pl.when(me == 0)
    def _():
        for e in range(count):
            lo[e] = jnp.zeros(lo.shape[1:], lo.dtype)

    @pl.when(me == n_energy - 1)
    def _():
        for e in range(count):
            up[count + e] = jnp.zeros(up.shape[1:], up.dtype)

    def stage_own(e, carry):
        block = green_ref[e]
        lo[count + e] = block
        up[e] = block
        own_t[e, 0] = block[0].T
        own_t[e, 1] = block[1].T
        return carry

    lax.fori_loop(0, count, stage_own, 0)

    offs = [off_ref[k] for k in range(noff)]

    def first_of(value):
        found = jnp.int32(noff - 1)
        for k in range(noff - 2, -1, -1):
            found = jnp.where(offs[k] == value, jnp.int32(k), found)
        return found

    low_slot, high_slot = first_of(-count), first_of(count)
    slots = [low_slot, high_slot]
    last = jnp.int32(-1)
    for _ in range(noff - 2):
        found = jnp.int32(noff - 1)
        for k in range(noff - 1, -1, -1):
            fits = jnp.logical_and(jnp.logical_and(k != low_slot, k != high_slot), k > last)
            found = jnp.where(fits, jnp.int32(k), found)
        slots.append(found)
        last = found
    positive = []
    for s, k in enumerate(slots):
        w = off_ref[k]
        n = occ_ref[k]
        sign = jnp.where(w > 0, jnp.float32(1.0), jnp.float32(0.0))
        positive.append(sign)
        reach[s] = jnp.where(w > 0, w, -w)
        coef[s] = n + 1.0 - sign
        coef[noff + s] = n + sign
        v = coup_ref[0, k]
        real, imag = vertex_ref[v, 0], vertex_ref[v, 1]
        wide[s, 0:nb, 0:nb] = real
        wide[s, 0:nb, nb:2 * nb] = -imag
        wide[s, nb:2 * nb, 0:nb] = imag
        wide[s, nb:2 * nb, nb:2 * nb] = real
        real_t, imag_t = real.T, imag.T
        wide_t[s, 0:nb, 0:nb] = real_t
        wide_t[s, 0:nb, nb:2 * nb] = -imag_t
        wide_t[s, nb:2 * nb, 0:nb] = imag_t
        wide_t[s, nb:2 * nb, nb:2 * nb] = real_t

    def clear(i, carry):
        acc[i] = jnp.zeros(acc.shape[1:], F32)
        return carry

    lax.fori_loop(0, acc.shape[0], clear, 0)

    def place(bit):
        return layer if bit == 0 else lax.div(me, bit) % 2

    def region(s, m):
        start = jnp.int32(0)
        for pair, parts, split, size, after in plan[:s]:
            if split:
                start = start + place(pair[m % 2]) * after
        return start

    def rows_at(start, size):
        return pl.ds(pl.multiple_of(start, ALIGN), size)

    def target(bit, r):
        return (me, lax.rem(layer + r, n_layer)) if bit == 0 else (flipped(bit), layer)

    def sum_copy(s, m, r):
        pair, parts, split, size, after = plan[s]
        bit = pair[m % 2]
        start = region(s, m)
        if split:
            mine = lax.rem(layer + r, n_layer) if bit == 0 else 1 - place(bit)
            start = start + mine * after
        return pltpu.make_async_remote_copy(
            src_ref=part.at[m, rows_at(start, after)], dst_ref=landing[s].at[m, r - 1],
            send_sem=sums_send[s].at[m, r - 1], recv_sem=sums_recv[s].at[m, r - 1],
            device_id=target(bit, r), device_id_type=MESH)

    def spread_copy(s, m, r):
        pair, parts, split, size, after = plan[s]
        where = rows_at(region(s + 1, m), after)
        return pltpu.make_async_remote_copy(
            src_ref=full.at[m, where], dst_ref=full.at[m, where],
            send_sem=spread_send[s].at[m, r - 1], recv_sem=spread_recv[s].at[m, r - 1],
            device_id=target(pair[m % 2], r), device_id_type=MESH)

    steps = [(sum_copy, s) for s in range(stages)]
    steps += [(spread_copy, s) for s in range(stages - 1, -1, -1) if plan[s][2]]

    def begin(i, m):
        make, s = steps[i]
        for r in range(1, plan[s][1]):
            make(s, m, r).start()

    def finish(i, m):
        make, s = steps[i]
        pair, parts, split, size, after = plan[s]
        for r in range(1, parts):
            make(s, m, r).wait()
        if make is sum_copy:
            where = rows_at(region(s + 1, m), after)
            total = part[m, where].astype(F32)
            for r in range(1, parts):
                total = total + landing[s][m, r - 1].astype(F32)
            if s == stages - 1:
                full[m, where] = total.astype(BF16)
            else:
                part[m, where] = total.astype(BF16)

    @pl.when(me < n_energy - 1)
    def _():
        for e in range(count):
            send_prev(e).wait_recv()

    for q in range(nq):
        w = reach[0] if q == 0 else reach[q + 1]

        def polar_rows(i, carry, q=q, w=w):
            rows = pl.ds(pl.multiple_of(i * ROWS, ROWS), ROWS)
            real = jnp.zeros((ROWS, nb), F32)
            imag = jnp.zeros((ROWS, nb), F32)
            for e in range(count):
                a_real = own_t[e, 0, rows].astype(F32)
                a_imag = own_t[e, 1, rows].astype(F32)
                b_real = up[e + w, 0, rows].astype(F32)
                b_imag = up[e + w, 1, rows].astype(F32)
                real = real + a_real * b_real - a_imag * b_imag
                imag = imag + a_real * b_imag + a_imag * b_real
            part[q, rows] = real.astype(BF16)
            part[q, pl.ds(pl.multiple_of(nb + i * ROWS, ROWS), ROWS)] = imag.astype(BF16)
            return carry

        lax.fori_loop(0, nb // ROWS, polar_rows, 0)
        begin(0, q)

    @pl.when(me > 0)
    def _():
        for e in range(count):
            send_next(e).wait_recv()

    pairs = count // 2
    units = noff * pairs

    def unit(i, carry):
        s, p = lax.div(i, pairs), lax.rem(i, pairs)
        w, c_low, c_up = reach[s], coef[s], coef[noff + s]
        for j in range(2):
            e = 2 * p + j
            for c in range(2):
                below = lo[count + e - w, c].astype(F32)
                above = up[e + w, c].astype(F32)
                mix[c * nb:(c + 1) * nb, j * nb:(j + 1) * nb] = (c_low * below + c_up * above).astype(BF16)
        product = jnp.dot(wide[s], mix[...], preferred_element_type=F32).astype(BF16)
        for j in range(2):
            for c in range(2):
                half[j * nb:(j + 1) * nb, c * nb:(c + 1) * nb] = product[c * nb:(c + 1) * nb, j * nb:(j + 1) * nb]
        acc[p] += jnp.dot(half[...], wide_t[s], preferred_element_type=F32)
        for step in range(min(len(steps), units)):
            @pl.when(i == step)
            def _(step=step):
                for m in range(nq):
                    finish(step, m)
                    if step + 1 < len(steps):
                        begin(step + 1, m)
        return carry

    lax.fori_loop(0, units, unit, 0)
    for step in range(units, len(steps)):
        for m in range(nq):
            finish(step, m)
            if step + 1 < len(steps):
                begin(step + 1, m)

    for s, k in enumerate(slots):
        f_real, f_imag = free_ref[k, 0], free_ref[k, 1]
        mix[0:nb, 0:nb] = f_real
        mix[0:nb, nb:2 * nb] = f_imag
        mix[nb:2 * nb, 0:nb] = -f_imag
        mix[nb:2 * nb, nb:2 * nb] = f_real
        q = 0 if s < 2 else s - 1
        for c in range(2):
            straight = full[q, c * nb:(c + 1) * nb]
            if s == 0:
                chosen = straight
            elif s == 1:
                chosen = straight.T
            else:
                turned = straight.T.astype(F32)
                chosen = (positive[s] * turned + (1.0 - positive[s]) * straight.astype(F32)).astype(BF16)
            half[0:nb, c * nb:(c + 1) * nb] = chosen
        magnon = jnp.dot(half[0:nb], mix[...], preferred_element_type=F32).astype(BF16).astype(F32)
        if s == 1:
            mag[0] += magnon
        else:
            mag[q] = magnon

    for e in range(count):
        def out_rows(i, carry, e=e):
            rows = pl.ds(pl.multiple_of(i * ROWS, ROWS), ROWS)
            base = pl.ds(pl.multiple_of((e % 2) * nb + i * ROWS, ROWS), ROWS)
            real = acc[e // 2, base, 0:nb]
            imag = acc[e // 2, base, nb:2 * nb]
            for q in range(nq):
                w = reach[0] if q == 0 else reach[q + 1]
                s_real = lo[count + e - w, 0, rows].astype(F32) + up[e + w, 0, rows].astype(F32)
                s_imag = lo[count + e - w, 1, rows].astype(F32) + up[e + w, 1, rows].astype(F32)
                m_real = mag[q, rows, 0:nb]
                m_imag = mag[q, rows, nb:2 * nb]
                real = real + m_real * s_real - m_imag * s_imag
                imag = imag + m_real * s_imag + m_imag * s_real
            out_ref[e, 0, 0, rows] = real.astype(BF16)
            out_ref[e, 0, 1, rows] = imag.astype(BF16)
            return carry

        lax.fori_loop(0, nb // ROWS, out_rows, 0)

    @pl.when(me > 0)
    def _():
        for e in range(count):
            send_prev(e).wait_send()

    @pl.when(me < n_energy - 1)
    def _():
        for e in range(count):
            send_next(e).wait_send()


def per_device(n_energy, n_layer, green_blocks, offsets, occupation, coupling, vertex, magnon_free):
    count, _, _, nb, _ = green_blocks.shape
    noff = offsets.shape[0]
    nq = noff - 1
    plan = reduction_plan(n_energy, n_layer, 2 * nb)
    smem = pl.BlockSpec(memory_space=pltpu.SMEM)
    vmem = pl.BlockSpec(memory_space=pltpu.VMEM)
    dma = pltpu.SemaphoreType.DMA
    scratch = [
        pltpu.VMEM((2 * count, 2, nb, nb), BF16),
        pltpu.VMEM((2 * count, 2, nb, nb), BF16),
        pltpu.VMEM((count, 2, nb, nb), BF16),
        pltpu.VMEM((noff, 2 * nb, 2 * nb), BF16),
        pltpu.VMEM((noff, 2 * nb, 2 * nb), BF16),
        pltpu.VMEM((count // 2, 2 * nb, 2 * nb), F32),
        pltpu.VMEM((2 * nb, 2 * nb), BF16),
        pltpu.VMEM((2 * nb, 2 * nb), BF16),
        pltpu.VMEM((nq, 2 * nb, nb), BF16),
        pltpu.VMEM((nq, 2 * nb, nb), BF16),
        pltpu.VMEM((nq, nb, 2 * nb), F32),
        pltpu.SMEM((noff,), jnp.int32),
        pltpu.SMEM((2 * noff,), F32),
    ]
    scratch += [pltpu.VMEM((nq, parts - 1, after, nb), BF16) for _, parts, _, _, after in plan]
    scratch += [dma((2, count)), dma((2, count))]
    for _ in range(4):
        scratch += [dma((nq, parts - 1)) for _, parts, _, _, _ in plan]
    flops = 16 * count * noff * 2 * nb ** 3
    return pl.pallas_call(
        functools.partial(kernel, n_energy, n_layer, plan),
        out_shape=jax.ShapeDtypeStruct(green_blocks.shape, BF16),
        in_specs=[smem, smem, smem, vmem, vmem, vmem],
        out_specs=vmem,
        scratch_shapes=scratch,
        compiler_params=pltpu.CompilerParams(
            collective_id=0, has_side_effects=True, vmem_limit_bytes=60 * 1024 * 1024),
        cost_estimate=pl.CostEstimate(
            flops=flops, bytes_accessed=4 * green_blocks.size * 2, transcendentals=0),
    )(offsets, occupation, coupling, green_blocks.reshape(count, 2, nb, nb), vertex, magnon_free)


def solution(mesh):
    placed = (P("energy", "layer", None, None, None), P(), P(), P("layer", None), P(), P())
    return jax.shard_map(
        functools.partial(per_device, mesh.shape["energy"], mesh.shape["layer"]),
        mesh=mesh,
        in_specs=placed,
        out_specs=P("energy", "layer", None, None, None),
        check_vma=False,
    )
```

time: 317 us -> 114 us (0.36)
  blocking collectives: 141 us -> 0 us
  Pallas kernels: 0 us -> 110 us
  local copies, waits for them, and re-layouts: 64 us -> 3.31 us
  other arithmetic: 56.9 us -> 0 us
  matrix products: 48.3 us -> 0 us
  starting transfers between devices: 5.18 us -> 0 us
    psum x1 -> x0, blocking collectives: 141 us -> none  [per_device(): lax.psum(partial_polar, ('energy', 'layer')).astype(jnp.bfloat16)]
    pallas_call x0 -> x1, Pallas kernels: none -> 110 us  [per_device(): pl.pallas_call(functools.partial(kernel, n_energy, n_layer, plan), out_sh...]
    dot_general x12 -> x0, matrix products: 48.3 us -> none  [product(): jnp.einsum(pattern, first, second, preferred_element_type=jnp.float32)]
    gather x6 -> x0, local copies, waits for them, and re-layouts: 47 us -> none  [the longest x2 21.3 us: per_device(): below = jnp.take(padded, local_index + count - offsets[None, :], axis=0)]
    reduce_sum x2 -> x0, other arithmetic: 18 us -> none  [the longest x1 9.32 us: per_device(): jnp.sum(own_wide[:, :, :, 0] * flipped[:, :, :, 0] - own_wide[:, :, :, 1]...]
    convert_element_type x2 -> x0, other arithmetic: 14.8 us -> none  [the longest x1 14.5 us: per_device(): (weights * below_wide + (weights + 1.0) * above_wide).astype(jnp.bfloat16)]
    transpose x1 -> x0, other arithmetic: 11.5 us -> none  [per_device(): flipped = jnp.swapaxes(above_wide, -1, -2)]
    mul x4 -> x0, local copies, waits for them, and re-layouts: 11.3 us -> none  [the longest x2 5.65 us: per_device(): magnon_wide[None, :, None, 0] * summed[:, :, :, 0]]
  transfers between devices with their start and end apart: 2 -> 0, of which waited for: 0 -> 0; matrix products, arithmetic and copies ran while one was open for 3% -> 0% of each run, Pallas kernels for 0% -> 0%
where the time goes in v1:
time: 114 us; the launch traced here: 113 us
  Pallas kernels  110 us (96%)
  local copies, waits for them, and re-layouts  3.31 us (3%)
    pallas_call x1, Pallas kernels, per_device(): pl.pallas_call(functools.partial(kernel, n_energy, n_layer, plan), out_sh...  110 us
    unnamed x1, local copies, waits for them, and re-layouts  3.31 us

profile of v1, /device:TPU:0, one launch (start us, length us, event | category | flops | bytes accessed | tf_op | source)
XLA Modules:
  0.0 113.5 jit_solution(8262617100341793702)
XLA Ops:
  0.0 110.2 %shard_map.64 = bf16[4,1,2,384,384]{4,3,2,1,0:T(8,128)(2,1)} custom-call(s32[4]{0:T(128)} %off_ref.1, f32[4]{0:T(128)} %occ_ref.1, s32[1,4]{1,0:T(1,128)} %coup_ref.1, bf16[4,2,384,384]{3,2,1,0:T(8,128)(2,1)} %bitcast.1, bf16[4,2,384,384]{3,2,1,0:T(8,128)(2,1)} %vertex_ref.1, bf16[4,2,384,384]{3,2,1,0:T(8,128)(2,1)} %free_ref.1), custom_call_target="tpu_custom_call" | custom-call | flops 28991029248 | bytes 9437184 | tf_op jit(solution)/shard_map/pallas_call | solution.py:369
  110.2 3.3 %copy.8 = bf16[4,1,2,384,384]{4,3,2,1,0:T(8,128)(2,1)} copy(bf16[4,1,2,384,384]{4,3,2,1,0:T(8,128)(2,1)} %shard_map.64) | data formatting | bytes 4718592

commit v2 on v1

--- a/solution.py
+++ b/solution.py
@@ -11,6 +11,7 @@
 F32 = jnp.float32
 BF16 = jnp.bfloat16
 ROWS = 32
+AHEAD = 3
 ALIGN = 16
 
 
@@ -22,10 +23,10 @@
         bit *= 2
     kinds = [[1, 1]] if n_energy > 1 else []
     if bits:
-        kinds.append([bits[-1], bits[0]])
+        kinds.append([bits[-1], bits[-1]])
     kinds.append([0, 0])
     for i in range(1, len(bits)):
-        kinds.append([bits[-1 - i], bits[i]])
+        kinds.append([bits[-1 - i], bits[-1 - i]])
     plan = []
     size = rows
     for pair in kinds:
@@ -42,7 +43,7 @@
 def kernel(
     n_energy, n_layer, plan,
     off_ref, occ_ref, coup_ref, green_ref, vertex_ref, free_ref, out_ref,
-    lo, up, own_t, wide, wide_t, acc, mix, half, part, full, mag, reach, coef, *rest,
+    lo, up, turned, wide, wide_t, acc, mix, half, part, full, mag, reach, coef, *rest,
 ):
     count = green_ref.shape[0]
     nb = green_ref.shape[-1]
@@ -86,15 +87,33 @@
             src_ref=green_ref.at[e], dst_ref=up.at[count + e], send_sem=halo_send.at[1, e],
             recv_sem=halo_recv.at[1, e], device_id=(me - 1, layer), device_id_type=MESH)
 
-    @pl.when(me > 0)
-    def _():
-        for e in range(count):
-            send_prev(e).start()
-
-    @pl.when(me < n_energy - 1)
-    def _():
-        for e in range(count):
-            send_next(e).start()
+    early = count // 2
+    prev_order = [list(range(early)), list(range(early, count))]
+    next_order = [list(range(early, count)), list(range(early))]
+
+    def halo(part_of, act):
+        @pl.when(me > 0)
+        def _():
+            for e in prev_order[part_of]:
+                getattr(send_prev(e), act)()
+
+        @pl.when(me < n_energy - 1)
+        def _():
+            for e in next_order[part_of]:
+                getattr(send_next(e), act)()
+
+    def halo_arrived(part_of):
+        @pl.when(me < n_energy - 1)
+        def _():
+            for e in prev_order[part_of]:
+                send_prev(e).wait_recv()
+
+        @pl.when(me > 0)
+        def _():
+            for e in next_order[part_of]:
+                send_next(e).wait_recv()
+
+    halo(0, "start")
 
     @pl.when(me == 0)
     def _():
@@ -110,8 +129,8 @@
         block = green_ref[e]
         lo[count + e] = block
         up[e] = block
-        own_t[e, 0] = block[0].T
-        own_t[e, 1] = block[1].T
+        turned[count - early + e, 0] = block[0].T
+        turned[count - early + e, 1] = block[1].T
         return carry
 
     lax.fori_loop(0, count, stage_own, 0)
@@ -140,7 +159,7 @@
         n = occ_ref[k]
         sign = jnp.where(w > 0, jnp.float32(1.0), jnp.float32(0.0))
         positive.append(sign)
-        reach[s] = jnp.where(w > 0, w, -w)
+        reach[s] = jnp.clip(jnp.where(w > 0, w, -w), 1, count)
         coef[s] = n + 1.0 - sign
         coef[noff + s] = n + sign
         v = coup_ref[0, k]
@@ -220,23 +239,31 @@
             else:
                 part[m, where] = total.astype(BF16)
 
-    @pl.when(me < n_energy - 1)
-    def _():
-        for e in range(count):
-            send_prev(e).wait_recv()
+    halo(0, "wait_send")
+    halo(1, "start")
+    halo_arrived(0)
+    for i in range(count - early):
+        turned[i, 0] = lo[early + i, 0].T
+        turned[i, 1] = lo[early + i, 1].T
 
     for q in range(nq):
-        w = reach[0] if q == 0 else reach[q + 1]
+        w = count if q == 0 else reach[q + 1]
 
         def polar_rows(i, carry, q=q, w=w):
             rows = pl.ds(pl.multiple_of(i * ROWS, ROWS), ROWS)
             real = jnp.zeros((ROWS, nb), F32)
             imag = jnp.zeros((ROWS, nb), F32)
-            for e in range(count):
-                a_real = own_t[e, 0, rows].astype(F32)
-                a_imag = own_t[e, 1, rows].astype(F32)
-                b_real = up[e + w, 0, rows].astype(F32)
-                b_imag = up[e + w, 1, rows].astype(F32)
+            for f in range(early, count + early):
+                b_real, b_imag = up[f, 0, rows], up[f, 1, rows]
+                at = count - early + f - w
+                if f > count and q > 0:
+                    inside = w <= f - count
+                    b_real = jnp.where(inside, up[f - count, 0, rows].astype(F32), b_real.astype(F32))
+                    b_imag = jnp.where(inside, up[f - count, 1, rows].astype(F32), b_imag.astype(F32))
+                    at = jnp.where(inside, at - count, at)
+                b_real, b_imag = b_real.astype(F32), b_imag.astype(F32)
+                a_real = turned[at, 0, rows].astype(F32)
+                a_imag = turned[at, 1, rows].astype(F32)
                 real = real + a_real * b_real - a_imag * b_imag
                 imag = imag + a_real * b_imag + a_imag * b_real
             part[q, rows] = real.astype(BF16)
@@ -246,10 +273,16 @@
         lax.fori_loop(0, nb // ROWS, polar_rows, 0)
         begin(0, q)
 
-    @pl.when(me > 0)
-    def _():
-        for e in range(count):
-            send_next(e).wait_recv()
+    def advance(step):
+        for m in range(nq):
+            finish(step, m)
+            if step + 1 < len(steps):
+                begin(step + 1, m)
+
+    ahead = min(AHEAD, len(steps))
+    for step in range(ahead):
+        advance(step)
+    halo_arrived(1)
 
     pairs = count // 2
     units = noff * pairs
@@ -268,21 +301,15 @@
             for c in range(2):
                 half[j * nb:(j + 1) * nb, c * nb:(c + 1) * nb] = product[c * nb:(c + 1) * nb, j * nb:(j + 1) * nb]
         acc[p] += jnp.dot(half[...], wide_t[s], preferred_element_type=F32)
-        for step in range(min(len(steps), units)):
-            @pl.when(i == step)
+        for step in range(ahead, min(len(steps), ahead + units)):
+            @pl.when(i == step - ahead)
             def _(step=step):
-                for m in range(nq):
-                    finish(step, m)
-                    if step + 1 < len(steps):
-                        begin(step + 1, m)
+                advance(step)
         return carry
 
     lax.fori_loop(0, units, unit, 0)
-    for step in range(units, len(steps)):
-        for m in range(nq):
-            finish(step, m)
-            if step + 1 < len(steps):
-                begin(step + 1, m)
+    for step in range(ahead + units, len(steps)):
+        advance(step)
 
     for s, k in enumerate(slots):
         f_real, f_imag = free_ref[k, 0], free_ref[k, 1]
@@ -298,8 +325,8 @@
             elif s == 1:
                 chosen = straight.T
             else:
-                turned = straight.T.astype(F32)
-                chosen = (positive[s] * turned + (1.0 - positive[s]) * straight.astype(F32)).astype(BF16)
+                flip = straight.T.astype(F32)
+                chosen = (positive[s] * flip + (1.0 - positive[s]) * straight.astype(F32)).astype(BF16)
             half[0:nb, c * nb:(c + 1) * nb] = chosen
         magnon = jnp.dot(half[0:nb], mix[...], preferred_element_type=F32).astype(BF16).astype(F32)
         if s == 1:
@@ -327,15 +354,7 @@
 
         lax.fori_loop(0, nb // ROWS, out_rows, 0)
 
-    @pl.when(me > 0)
-    def _():
-        for e in range(count):
-            send_prev(e).wait_send()
-
-    @pl.when(me < n_energy - 1)
-    def _():
-        for e in range(count):
-            send_next(e).wait_send()
+    halo(1, "wait_send")
 
 
 def per_device(n_energy, n_layer, green_blocks, offsets, occupation, coupling, vertex, magnon_free):
@@ -349,7 +368,7 @@
     scratch = [
         pltpu.VMEM((2 * count, 2, nb, nb), BF16),
         pltpu.VMEM((2 * count, 2, nb, nb), BF16),
-        pltpu.VMEM((count, 2, nb, nb), BF16),
+        pltpu.VMEM((2 * count - count // 2, 2, nb, nb), BF16),
         pltpu.VMEM((noff, 2 * nb, 2 * nb), BF16),
         pltpu.VMEM((noff, 2 * nb, 2 * nb), BF16),
         pltpu.VMEM((count // 2, 2 * nb, 2 * nb), F32),

time: 114 us -> 108 us (0.947)
  Pallas kernels: 110 us -> 105 us
    pallas_call x1, Pallas kernels: 110 us -> 105 us  [per_device(): pl.pallas_call(functools.partial(kernel, n_energy, n_layer, plan), out_sh...]
where the time goes in v2:
time: 108 us
  Pallas kernels  105 us (97%)
  local copies, waits for them, and re-layouts  3.31 us (3%)
    pallas_call x1, Pallas kernels, per_device(): pl.pallas_call(functools.partial(kernel, n_energy, n_layer, plan), out_sh...  105 us
    unnamed x1, local copies, waits for them, and re-layouts  3.31 us

profile of v2, /device:TPU:0, one launch (start us, length us, event | category | flops | bytes accessed | tf_op | source)
XLA Modules:
  0.0 108.1 jit_solution(4922654784644932388)
XLA Ops:
  0.0 104.8 %shard_map.64 = bf16[4,1,2,384,384]{4,3,2,1,0:T(8,128)(2,1)} custom-call(s32[4]{0:T(128)} %off_ref.1, f32[4]{0:T(128)} %occ_ref.1, s32[1,4]{1,0:T(1,128)} %coup_ref.1, bf16[4,2,384,384]{3,2,1,0:T(8,128)(2,1)} %bitcast.1, bf16[4,2,384,384]{3,2,1,0:T(8,128)(2,1)} %vertex_ref.1, bf16[4,2,384,384]{3,2,1,0:T(8,128)(2,1)} %free_ref.1), custom_call_target="tpu_custom_call" | custom-call | flops 28991029248 | bytes 9437184 | tf_op jit(solution)/shard_map/pallas_call | solution.py:388
  104.8 3.3 %copy.8 = bf16[4,1,2,384,384]{4,3,2,1,0:T(8,128)(2,1)} copy(bf16[4,1,2,384,384]{4,3,2,1,0:T(8,128)(2,1)} %shard_map.64) | data formatting | bytes 4718592

commit v3 on v2

--- a/solution.py
+++ b/solution.py
@@ -12,6 +12,8 @@
 BF16 = jnp.bfloat16
 ROWS = 32
 AHEAD = 3
+LANES = 128
+WIDTH = 256
 ALIGN = 16
 
 
@@ -290,17 +292,29 @@
     def unit(i, carry):
         s, p = lax.div(i, pairs), lax.rem(i, pairs)
         w, c_low, c_up = reach[s], coef[s], coef[noff + s]
-        for j in range(2):
-            e = 2 * p + j
-            for c in range(2):
-                below = lo[count + e - w, c].astype(F32)
-                above = up[e + w, c].astype(F32)
-                mix[c * nb:(c + 1) * nb, j * nb:(j + 1) * nb] = (c_low * below + c_up * above).astype(BF16)
-        product = jnp.dot(wide[s], mix[...], preferred_element_type=F32).astype(BF16)
-        for j in range(2):
-            for c in range(2):
-                half[j * nb:(j + 1) * nb, c * nb:(c + 1) * nb] = product[c * nb:(c + 1) * nb, j * nb:(j + 1) * nb]
-        acc[p] += jnp.dot(half[...], wide_t[s], preferred_element_type=F32)
+
+        def mix_rows(r, carry):
+            rows = pl.ds(pl.multiple_of(r * ROWS, ROWS), ROWS)
+            for j in range(2):
+                e = 2 * p + j
+                for c in range(2):
+                    below = lo[count + e - w, c, rows].astype(F32)
+                    above = up[e + w, c, rows].astype(F32)
+                    to = pl.ds(pl.multiple_of(c * nb + r * ROWS, ROWS), ROWS)
+                    mix[to, j * nb:(j + 1) * nb] = (c_low * below + c_up * above).astype(BF16)
+            return carry
+
+        lax.fori_loop(0, nb // ROWS, mix_rows, 0)
+        for at in range(0, 2 * nb, WIDTH):
+            product = jnp.dot(wide[s], mix[:, at:at + WIDTH], preferred_element_type=F32).astype(BF16)
+            for g in range(at, at + WIDTH, LANES):
+                j, col = g // nb, g % nb
+                for c in range(2):
+                    half[j * nb:(j + 1) * nb, c * nb + col:c * nb + col + LANES] = product[
+                        c * nb:(c + 1) * nb, g - at:g - at + LANES]
+        for at in range(0, 2 * nb, WIDTH):
+            acc[p, :, at:at + WIDTH] += jnp.dot(
+                half[...], wide_t[s, :, at:at + WIDTH], preferred_element_type=F32)
         for step in range(ahead, min(len(steps), ahead + units)):
             @pl.when(i == step - ahead)
             def _(step=step):

time: 108 us -> 111 us (1.028)
  Pallas kernels: 105 us -> 107 us
    pallas_call x1, Pallas kernels: 105 us -> 107 us  [per_device(): pl.pallas_call(functools.partial(kernel, n_energy, n_layer, plan), out_sh...]
where the time goes in v3:
time: 111 us; the launch traced here: 110 us
  Pallas kernels  107 us (96%)
  local copies, waits for them, and re-layouts  3.31 us (3%)
    pallas_call x1, Pallas kernels, per_device(): pl.pallas_call(functools.partial(kernel, n_energy, n_layer, plan), out_sh...  107 us
    unnamed x1, local copies, waits for them, and re-layouts  3.31 us

profile of v3, /device:TPU:0, one launch (start us, length us, event | category | flops | bytes accessed | tf_op | source)
XLA Modules:
  0.0 110.4 jit_solution(15756581090456070817)
XLA Ops:
  0.0 107.0 %shard_map.64 = bf16[4,1,2,384,384]{4,3,2,1,0:T(8,128)(2,1)} custom-call(s32[4]{0:T(128)} %off_ref.1, f32[4]{0:T(128)} %occ_ref.1, s32[1,4]{1,0:T(1,128)} %coup_ref.1, bf16[4,2,384,384]{3,2,1,0:T(8,128)(2,1)} %bitcast.1, bf16[4,2,384,384]{3,2,1,0:T(8,128)(2,1)} %vertex_ref.1, bf16[4,2,384,384]{3,2,1,0:T(8,128)(2,1)} %free_ref.1), custom_call_target="tpu_custom_call" | custom-call | flops 28991029248 | bytes 9437184 | tf_op jit(solution)/shard_map/pallas_call | solution.py:402
  107.0 3.3 %copy.8 = bf16[4,1,2,384,384]{4,3,2,1,0:T(8,128)(2,1)} copy(bf16[4,1,2,384,384]{4,3,2,1,0:T(8,128)(2,1)} %shard_map.64) | data formatting | bytes 4718592
